TPU v7x, 256 devices: a whole 4x4x8 slice. The times are simulated.
256 devices in a mesh: leaf: 32 (over z, y), sub: 8 (over x, core).
Axes of the slice: x: 4, y: 4, z: 8, core: 2. Of those that a mesh axis runs over, the one named last changes fastest.
Arguments:
- bottom_coeffs: bfloat16 [8192, 64, 64], P(('leaf', 'sub')), may hold values from -6 to 6
- local_transfer: bfloat16 [256, 63, 64, 64], P(('leaf', 'sub')), may hold values from -0.5 to 0.5
- coarse_transfer: bfloat16 [32, 6, 64, 64], P('leaf'), may hold values from -0.5 to 0.5
- local_coupling: bfloat16 [256, 63, 16, 64, 64], P(('leaf', 'sub')), may hold values from -0.1875 to 0.1875
- local_partners: int32 [256, 63, 16], P(('leaf', 'sub')), may hold values from -32 to 32, as said below
- local_counts: int32 [256, 63], P(('leaf', 'sub')), may hold values from 1 to 16
- coarse_coupling: bfloat16 [32, 7, 16, 64, 64], P('leaf'), may hold values from -0.1875 to 0.1875
- coarse_partners: int32 [32, 7, 16], P('leaf'), may hold values from 0 to 127, as said below
- coarse_counts: int32 [32, 7], P('leaf'), may hold values from 1 to 16
Outputs:
- far_field: bfloat16 [8192, 64, 64], P(('leaf', 'sub'))
Inputs may be any that keep to these rules, and one draw needn't show every extreme that they name: `local_partners`: A cluster at a level with n clusters a device has offsets from -n to n. `coarse_partners`: A partner of a coarse node at depth t lies in the level with 32 * 2^t clusters.
All inputs are finite; a program needn't handle non-finite values.
Results may differ from a plain program's by a relative error of at most 0.023.
Values may be sent and summed in bfloat16 or wider, within the bound.
A program may use at most 128 MiB of HBM per device.

v0:
```python
import jax
import jax.numpy as jnp
import numpy as np
from jax import lax
from jax.sharding import PartitionSpec as P


def with_halo(array, sides, width):
    for axis, dim in sides:
        peers, length = (lax.axis_size(axis), array.shape[dim])
        up = [(i, (i + 1) % peers) for i in range(peers - 1)]
        down = [(j, i) for i, j in up]
        last = lax.slice_in_dim(array, length - width, length, axis=dim)
        first = lax.slice_in_dim(array, 0, width, axis=dim)
        before = lax.ppermute(last, axis, up)
        after = lax.ppermute(first, axis, down)
        array = jnp.concatenate([before, array, after], axis=dim)
    return array


def lift_level(child_coeffs, child_transfer):
    products = jnp.einsum(
        "iab,ibq->iaq", child_transfer, child_coeffs, preferred_element_type=jnp.float32
    )
    paired = products.reshape((products.shape[0] // 2, 2) + products.shape[1:])
    return (paired[:, 0] + paired[:, 1]).astype(jnp.bfloat16)


def couple_level(source, where_from, counts, blocks):
    chosen = source[where_from]
    active = (jnp.arange(where_from.shape[1], dtype=jnp.int32)[None, :] < counts[:, None]).astype(
        source.dtype
    )
    chosen = chosen * active[:, :, None, None]
    return jnp.einsum("ikab,ikbq->iaq", blocks, chosen, preferred_element_type=jnp.float32)


def lower_level(coupled, spread, transfer):
    return (
        coupled + jnp.einsum("iba,ibq->iaq", transfer, spread, preferred_element_type=jnp.float32)
    ).astype(jnp.bfloat16)


def on_device(
    bottom_coeffs,
    local_transfer,
    coarse_transfer,
    local_coupling,
    local_partners,
    local_counts,
    coarse_coupling,
    coarse_partners,
    coarse_counts,
):
    clusters = bottom_coeffs.shape[0]
    transfer = local_transfer[0]
    coupling = local_coupling[0]
    partners = local_partners[0]
    counts = local_counts[0]
    widths = []
    n = clusters
    while n >= 1:
        widths.append(n)
        n = n // 2
    coeffs = {clusters: bottom_coeffs}
    for n in widths[1:]:
        coeffs[n] = lift_level(coeffs[2 * n], transfer[2 * n - 1 : 4 * n - 1])
    padded = {n: with_halo(coeffs[n], ((("leaf", "sub"), 0),), n) for n in widths}
    coupled = {}
    for n in widths:
        where_from = jnp.arange(n, dtype=jnp.int32)[:, None] + n + partners[n - 1 : 2 * n - 1]
        coupled[n] = couple_level(
            padded[n], where_from, counts[n - 1 : 2 * n - 1], coupling[n - 1 : 2 * n - 1]
        )
    group_coeffs, group_lifts = (
        lax.all_gather(coeffs[1], "sub", axis=0, tiled=True),
        lax.all_gather(transfer[0:1], "sub", axis=0, tiled=True),
    )
    group_size = lax.axis_size("sub")
    tree_depth = group_size.bit_length() - 1
    upper = {}
    children = group_coeffs
    child_transfer = group_lifts
    for t in range(tree_depth - 1, -1, -1):
        upper[t] = lift_level(children, child_transfer)
        children = upper[t]
        if t > 0:
            child_transfer = coarse_transfer[0, 2**t - 2 : 2 ** (t + 1) - 2]
    coarse_coeffs = jnp.concatenate([upper[t] for t in range(tree_depth)], axis=0)
    level_span = jnp.asarray(
        np.array([1 << s.bit_length() - 1 for s in range(1, group_size)], dtype=np.int32)
    )[:, None]
    partner_ids = coarse_partners[0]
    pool_slot = (
        partner_ids // level_span * (group_size - 1) + level_span + partner_ids % level_span - 1
    )
    pooled = lax.all_gather(coarse_coeffs, "leaf", axis=0, tiled=True)
    coarse_sums = couple_level(pooled, pool_slot, coarse_counts[0], coarse_coupling[0])
    values = coarse_sums[0:1].astype(jnp.bfloat16)
    for t in range(1, tree_depth):
        values = lower_level(
            coarse_sums[2**t - 1 : 2 ** (t + 1) - 1],
            jnp.repeat(values, 2, axis=0),
            coarse_transfer[0, 2**t - 2 : 2 ** (t + 1) - 2],
        )
    own_parent = lax.dynamic_slice_in_dim(values, lax.axis_index("sub") // 2, 1, 0)
    values = lower_level(coupled[1], own_parent, transfer[0:1])
    for n in widths[-2::-1]:
        values = lower_level(coupled[n], jnp.repeat(values, 2, axis=0), transfer[n - 1 : 2 * n - 1])
    return values


def solution(mesh):
    placed = (
        P(("leaf", "sub"), None, None),
        P(("leaf", "sub"), None, None, None),
        P("leaf", None, None, None),
        P(("leaf", "sub"), None, None, None, None),
        P(("leaf", "sub"), None, None),
        P(("leaf", "sub"), None),
        P("leaf", None, None, None, None),
        P("leaf", None, None),
        P("leaf", None),
    )
    return jax.shard_map(
        on_device,
        mesh=mesh,
        in_specs=placed,
        out_specs=P(("leaf", "sub"), None, None),
        check_vma=False,
    )
```

profile of v0, /device:TPU:127, one launch (start us, length us, event | category | flops | bytes accessed | tf_op | source)
XLA Modules:
  0.0 202.4 jit_solution(15050090385384982077)
XLA Ops:
  6.5 1.6 fusion.85
  8.2 0.9 fusion.163
  9.1 2.0 %copy.82 = f32[16,1,64,64]{2,3,0,1:T(8,128)} copy(f32[16,1,64,64]{3,2,1,0:T(8,128)} %get-tuple-element.8) | data formatting | bytes 524288
  11.1 1.0 copy.83
  12.1 1.3 fusion.92
  14.8 0.9 convolution_bitcast_fusion.4
  15.7 4.9 %collective-permute-start.10 = (bf16[1,64,64]{1,2,0:T(8,128)(2,1)S(1)}, bf16[1,64,64]{1,2,0:T(8,128)(2,1)}, u32[]{:S(2)}, u32[]{:S(2)}) collective-permute-start(bf16[1,64,64]{1,2,0:T(8,128)(2,1)S(1)} %fusion.178), channel_id=1, source_target_pairs={{0,1},{1,2},{2,3},{3,4},{4,5},{5,6},{6,7},{7,8},{8,9},{9,10},{10,1... | collective-permute-start | bytes 24584 | tf_op jit(solution)/shard_map/ppermute | solution.py:15
  20.6 1.9 collective-permute-start.11
  22.5 9.1 %collective-permute-start.8 = (bf16[2,64,64]{1,2,0:T(8,128)(2,1)}, bf16[2,64,64]{1,2,0:T(8,128)(2,1)}, u32[]{:S(2)}, u32[]{:S(2)}) collective-permute-start(bf16[2,64,64]{1,2,0:T(8,128)(2,1)} %fusion.132), channel_id=1, source_target_pairs={{0,1},{1,2},{2,3},{3,4},{4,5},{5,6},{6,7},{7,8},{8,9},{9,10},{10,1... | collective-permute-start | bytes 49160 | tf_op jit(solution)/shard_map/ppermute | solution.py:15
  31.6 1.9 collective-permute-start.9
  33.5 9.1 %collective-permute-start.6 = (bf16[4,64,64]{1,2,0:T(8,128)(2,1)S(1)}, bf16[4,64,64]{1,2,0:T(8,128)(2,1)}, u32[]{:S(2)}, u32[]{:S(2)}) collective-permute-start(bf16[4,64,64]{1,2,0:T(8,128)(2,1)S(1)} %fusion.118), channel_id=1, source_target_pairs={{0,1},{1,2},{2,3},{3,4},{4,5},{5,6},{6,7},{7,8},{8,9},{9,10},{10,1... | collective-permute-start | bytes 98312 | tf_op jit(solution)/shard_map/ppermute | solution.py:15
  42.7 9.9 %all-gather = bf16[8,1,64,64]{3,2,1,0:T(8,128)(2,1)S(1)} all-gather(bf16[1,1,64,64]{3,2,1,0:T(8,128)(2,1)S(1)} %copy.63), channel_id=2, replica_groups=mesh['leaf'=32,'sub'=8] {'sub'}, dimensions={0}, use_global_device_ids=true | all-gather | bytes 73728 | tf_op jit(solution)/shard_map/all_gather | solution.py:76
  52.6 13.1 %all-gather.1 = bf16[8,1,64,64]{3,2,1,0:T(8,128)(2,1)S(1)} all-gather(bf16[1,1,64,64]{3,2,1,0:T(8,128)(2,1)S(1)} %slice-done.2), channel_id=3, replica_groups=mesh['leaf'=32,'sub'=8] {'sub'}, dimensions={0}, use_global_device_ids=true | all-gather | bytes 73728 | tf_op jit(solution)/shard_map/all_gather | solution.py:77
  67.9 0.7 slice_bitcast_fusion.6
  68.6 0.7 slice_bitcast_fusion.7
  69.4 0.7 slice_bitcast_fusion.8
  70.1 1.1 fusion.156
  73.1 0.7 slice_bitcast_fusion.9
  73.9 0.7 slice_bitcast_fusion.10
  77.5 2.1 %collective-permute-start.7 = (bf16[4,64,64]{1,2,0:T(8,128)(2,1)S(1)}, bf16[4,64,64]{1,2,0:T(8,128)(2,1)S(1)}, u32[]{:S(2)}, u32[]{:S(2)}) collective-permute-start(bf16[4,64,64]{1,2,0:T(8,128)(2,1)S(1)} %fusion.118), channel_id=1, source_target_pairs={{1,0},{2,1},{3,2},{4,3},{5,4},{6,5},{7,6},{8,7},{9,8},{10,9},{11,1... | collective-permute-start | bytes 98312 | tf_op jit(solution)/shard_map/ppermute | solution.py:16
  79.6 8.9 %collective-permute-start.4 = (bf16[8,64,64]{1,2,0:T(8,128)(2,1)S(1)}, bf16[8,64,64]{1,2,0:T(8,128)(2,1)S(1)}, u32[]{:S(2)}, u32[]{:S(2)}) collective-permute-start(bf16[8,64,64]{1,2,0:T(8,128)(2,1)S(1)} %fusion.105), channel_id=1, source_target_pairs={{0,1},{1,2},{2,3},{3,4},{4,5},{5,6},{6,7},{7,8},{8,9},{9,10},{10,1... | collective-permute-start | bytes 196616 | tf_op jit(solution)/shard_map/ppermute | solution.py:15
  88.5 0.8 pad_maximum_fusion.6
  89.9 1.2 convolution_bitcast_fusion.6
  91.1 1.9 collective-permute-start.5
  93.1 9.1 %collective-permute-start.2 = (bf16[16,64,64]{1,2,0:T(8,128)(2,1)S(1)}, bf16[16,64,64]{1,2,0:T(8,128)(2,1)S(1)}, u32[]{:S(2)}, u32[]{:S(2)}) collective-permute-start(bf16[16,64,64]{1,2,0:T(8,128)(2,1)S(1)} %fusion.92), channel_id=1, source_target_pairs={{0,1},{1,2},{2,3},{3,4},{4,5},{5,6},{6,7},{7,8},{8,9},{9,10},{10,1... | collective-permute-start | bytes 393224 | tf_op jit(solution)/shard_map/ppermute | solution.py:15
  102.1 0.8 pad_maximum_fusion.5
  103.6 2.0 convolution_bitcast_fusion.5
  105.6 1.9 collective-permute-start.3
  107.5 9.1 %collective-permute-start = (bf16[32,64,64]{2,1,0:T(8,128)(2,1)}, bf16[32,64,64]{2,1,0:T(8,128)(2,1)}, u32[]{:S(2)}, u32[]{:S(2)}) collective-permute-start(bf16[32,64,64]{2,1,0:T(8,128)(2,1)} %param.10), channel_id=1, source_target_pairs={{0,1},{1,2},{2,3},{3,4},{4,5},{5,6},{6,7},{7,8},{8,9},{9,10},{10,1... | collective-permute-start | bytes 786440 | tf_op jit(solution)/shard_map/ppermute | solution.py:15
  116.6 0.9 pad_maximum_fusion.3
  117.5 1.7 gather_fusion.3
  119.2 2.7 %convolution_bitcast_fusion.1 = f32[4,64,64]{2,1,0:T(8,128)} fusion(bf16[1,63,16,64,64]{4,3,2,1,0:T(8,128)(2,1)} %param.13, bf16[4,16,64,64]{2,3,1,0:T(8,128)(2,1)} %bitcast.326, bf16[4,16]{1,0:T(4,128)(2,1)S(1)} %fusion.159), kind=kOutput, calls=%fused_computation.40 | convolution fusion | flops 33816576 | bytes 2162816 | tf_op jit(solution)/shard_map/ikab,ikbq->iaq/dot_general | solution.py:35
  121.9 2.1 %collective-permute-start.1 = (bf16[32,64,64]{2,1,0:T(8,128)(2,1)}, bf16[32,64,64]{2,1,0:T(8,128)(2,1)}, u32[]{:S(2)}, u32[]{:S(2)}) collective-permute-start(bf16[32,64,64]{2,1,0:T(8,128)(2,1)} %param.10), channel_id=1, source_target_pairs={{1,0},{2,1},{3,2},{4,3},{5,4},{6,5},{7,6},{8,7},{9,8},{10,9},{11,1... | collective-permute-start | bytes 786440 | tf_op jit(solution)/shard_map/ppermute | solution.py:16
  124.0 1.0 pad_maximum_fusion.2
  125.0 2.2 %gather_fusion.2 = bf16[128,64,64]{1,2,0:T(8,128)(2,1)} fusion(bf16[24,64,64]{1,2,0:T(8,128)(2,1)S(1)} %pad_maximum_fusion.2, s32[1024]{0:T(1024)S(1)} %pad_clamp_fusion.4), kind=kCustom, calls=%fused_computation.2 | custom fusion | bytes 2097664 | tf_op jit(solution)/shard_map/gather | solution.py:30
  127.2 3.8 %fusion.57 = f32[8,64,64]{2,1,0:T(8,128)} fusion(bf16[1,63,16,64,64]{4,3,2,1,0:T(8,128)(2,1)} %param.13, bf16[8,16,64,64]{2,3,1,0:T(8,128)(2,1)} %bitcast.323, bf16[8,16]{1,0:T(8,128)(2,1)S(1)} %fusion.153), kind=kOutput, calls=%fused_computation.34 | convolution fusion | flops 67633152 | bytes 4325632 | tf_op jit(solution)/shard_map/ikab,ikbq->iaq/dot_general | solution.py:35
  131.6 1.2 pad_maximum_fusion.1
  132.8 3.0 %gather_fusion.1 = bf16[256,64,64]{1,2,0:T(8,128)(2,1)} fusion(bf16[48,64,64]{1,2,0:T(8,128)(2,1)S(1)} %pad_maximum_fusion.1, s32[1024]{0:T(1024)S(1)} %pad_clamp_fusion.5), kind=kCustom, calls=%fused_computation.1 | custom fusion | bytes 4195328 | tf_op jit(solution)/shard_map/gather | solution.py:30
  135.9 10.3 %collective-permute-done.1 = bf16[32,64,64]{2,1,0:T(8,128)(2,1)} collective-permute-done((bf16[32,64,64]{2,1,0:T(8,128)(2,1)}, bf16[32,64,64]{2,1,0:T(8,128)(2,1)}, u32[]{:S(2)}, u32[]{:S(2)}) %collective-permute-start.1) | collective-permute-done | bytes 262176 | tf_op jit(solution)/shard_map/ppermute | solution.py:16
  146.2 1.7 pad_maximum_fusion
  147.9 13.4 %gather_fusion = bf16[512,64,64]{2,1,0:T(8,128)(2,1)} fusion(bf16[96,64,64]{2,1,0:T(8,128)(2,1)S(1)} %pad_maximum_fusion, s32[1024]{0:T(1024)S(1)} %pad_clamp_fusion.6), kind=kCustom, calls=%fused_computation | custom fusion | bytes 8390656 | tf_op jit(solution)/shard_map/gather | solution.py:30
  161.3 12.0 %copy.50 = bf16[32,16,64,64]{2,3,1,0:T(8,128)(2,1)} copy(bf16[32,16,64,64]{3,2,1,0:T(8,128)(2,1)} %bitcast.317) | data formatting | bytes 8388608 | tf_op jit(solution)/shard_map/gather | solution.py:30
  173.3 4.1 %gather_fusion.6 = bf16[112,64,64]{2,1,0:T(8,128)(2,1)} fusion(bf16[224,64,64]{2,1,0:T(8,128)(2,1)} %all-gather.4.cloned.1.call-done, s32[1024]{0:T(1024)S(1)} %copy-done.11), kind=kCustom, calls=%fused_computation.6 | custom fusion | bytes 1835456 | tf_op jit(solution)/shard_map/gather | solution.py:30
  177.4 3.9 %copy.72 = bf16[7,16,64,64]{2,3,1,0:T(8,128)(2,1)} copy(bf16[7,16,64,64]{3,2,1,0:T(8,128)(2,1)} %bitcast.320) | data formatting | bytes 1835008 | tf_op jit(solution)/shard_map/gather | solution.py:30
  181.3 2.3 %fusion.62 = f32[7,64,64]{1,2,0:T(8,128)S(1)} fusion(bf16[1,7,16,64,64]{4,3,2,1,0:T(8,128)(2,1)S(1)} %copy-done, bf16[7,16,64,64]{2,3,1,0:T(8,128)(2,1)} %copy.72, bf16[7,16]{1,0:T(8,128)(2,1)S(1)} %copy-done.15), kind=kOutput, calls=%fused_computation.35 | convolution fusion | flops 59179008 | bytes 1949920 | tf_op jit(solution)/shard_map/ikab,ikbq->iaq/dot_general | solution.py:35
  185.0 3.6 %fusion.52 = bf16[16,64,64]{1,2,0:T(8,128)(2,1)S(1)} fusion(f32[16,64,64]{2,1,0:T(8,128)S(1)} %fusion.96, bf16[1,63,16,64,64]{4,3,2,1,0:T(8,128)(2,1)} %param.13, bf16[16,16,64,64]{2,3,1,0:T(8,128)(2,1)S(1)} %bitcast.321, bf16[16,16]{1,0:T(8,128)(2,1)S(1)} %copy-done.13), kind=kOutput, calls=%fused_computation.32 | convolution fusion | flops 135397376 | bytes 6685184 | tf_op jit(solution)/shard_map/ikab,ikbq->iaq/dot_general | solution.py:35
  189.5 5.0 %fusion.32 = bf16[32,64,64]{1,2,0:T(8,128)(2,1)S(1)} fusion(f32[32,64,64]{2,1,0:T(8,128)S(1)} %fusion.83, bf16[1,63,16,64,64]{4,3,2,1,0:T(8,128)(2,1)} %param.13, bf16[32,16,64,64]{2,3,1,0:T(8,128)(2,1)S(1)} %bitcast.319, bf16[32,16]{1,0:T(8,128)(2,1)S(1)} %copy-done.12), kind=kOutput, calls=%fused_computation.28 | convolution fusion | flops 270794752 | bytes 13370368 | tf_op jit(solution)/shard_map/ikab,ikbq->iaq/dot_general | solution.py:35
  194.5 1.0 copy.73
  (135 shorter events, 12.4 us)
Async XLA Ops:
  6.5 174.8 %copy-start = (bf16[1,7,16,64,64]{4,3,2,1,0:T(8,128)(2,1)S(1)}, bf16[1,7,16,64,64]{4,3,2,1,0:T(8,128)(2,1)}, u32[]{:S(2)}) copy-start(bf16[1,7,16,64,64]{4,3,2,1,0:T(8,128)(2,1)} %param.16) | copy-start | bytes 2752516
  6.5 6.9 %copy-start.3 = (bf16[1,63,64,64]{3,2,1,0:T(8,128)(2,1)S(1)}, bf16[1,63,64,64]{3,2,1,0:T(8,128)(2,1)}, u32[]{:S(2)}) copy-start(bf16[1,63,64,64]{3,2,1,0:T(8,128)(2,1)} %param.11) | copy-start | bytes 1548292
  6.5 166.8 %all-gather.4.cloned.1.call-start = ((), (), s32[]{:S(2)}) async-start(), calls=%async_computation | async-start | bytes 3784704 | tf_op jit(solution)/shard_map/all_gather | solution.py:97
  8.2 44.4 %slice-start.2 = ((bf16[1,63,64,64]{3,2,1,0:T(8,128)(2,1)}), bf16[1,1,64,64]{3,2,1,0:T(8,128)(2,1)S(1)}, s32[]{:S(2)}) async-start(bf16[1,63,64,64]{3,2,1,0:T(8,128)(2,1)} %param.11), calls=%async_computation.3 | async-start | bytes 32768 | tf_op jit(solution)/shard_map/slice | solution.py:107
  11.1 55.0 %copy-start.5 = (bf16[1,6,64,64]{3,2,1,0:T(8,128)(2,1)S(1)}, bf16[1,6,64,64]{3,2,1,0:T(8,128)(2,1)}, u32[]{:S(2)}) copy-start(bf16[1,6,64,64]{3,2,1,0:T(8,128)(2,1)} %param.12) | copy-start | bytes 147460
  12.1 55.5 %copy-start.6 = (s32[1,63,16]{1,2,0:T(8,128)S(1)}, s32[1,63,16]{1,2,0:T(8,128)}, u32[]{:S(2)}) copy-start(s32[1,63,16]{1,2,0:T(8,128)} %param.14) | copy-start | bytes 12100
  12.1 58.0 %copy-start.14 = (s32[1,7,16]{2,0,1:T(1,128)S(1)}, s32[1,7,16]{2,0,1:T(1,128)}, u32[]{:S(2)}) copy-start(s32[1,7,16]{2,0,1:T(1,128)} %param.17) | copy-start | bytes 1348
  12.1 62.6 %copy-start.16 = (s32[1,7]{1,0:T(1,128)S(1)}, s32[1,7]{1,0:T(1,128)}, u32[]{:S(2)}) copy-start(s32[1,7]{1,0:T(1,128)} %param.18) | copy-start | bytes 88
  15.7 61.8 %collective-permute-start.10 = (bf16[1,64,64]{1,2,0:T(8,128)(2,1)S(1)}, bf16[1,64,64]{1,2,0:T(8,128)(2,1)}, u32[]{:S(2)}, u32[]{:S(2)}) collective-permute-start(bf16[1,64,64]{1,2,0:T(8,128)(2,1)S(1)} %fusion.178), channel_id=1, source_target_pairs={{0,1},{1,2},{2,3},{3,4},{4,5},{5,6},{6,7},{7,8},{8,9},{9,10},{10,1... | collective-permute-start | bytes 24584 | tf_op jit(solution)/shard_map/ppermute | solution.py:15
  20.6 59.0 %collective-permute-start.11 = (bf16[1,64,64]{1,2,0:T(8,128)(2,1)S(1)}, bf16[1,64,64]{1,2,0:T(8,128)(2,1)}, u32[]{:S(2)}, u32[]{:S(2)}) collective-permute-start(bf16[1,64,64]{1,2,0:T(8,128)(2,1)S(1)} %fusion.178), channel_id=1, source_target_pairs={{1,0},{2,1},{3,2},{4,3},{5,4},{6,5},{7,6},{8,7},{9,8},{10,9},{11,1... | collective-permute-start | bytes 24584 | tf_op jit(solution)/shard_map/ppermute | solution.py:16
  22.5 68.6 %collective-permute-start.8 = (bf16[2,64,64]{1,2,0:T(8,128)(2,1)}, bf16[2,64,64]{1,2,0:T(8,128)(2,1)}, u32[]{:S(2)}, u32[]{:S(2)}) collective-permute-start(bf16[2,64,64]{1,2,0:T(8,128)(2,1)} %fusion.132), channel_id=1, source_target_pairs={{0,1},{1,2},{2,3},{3,4},{4,5},{5,6},{6,7},{7,8},{8,9},{9,10},{10,1... | collective-permute-start | bytes 49160 | tf_op jit(solution)/shard_map/ppermute | solution.py:15
  31.6 61.5 %collective-permute-start.9 = (bf16[2,64,64]{1,2,0:T(8,128)(2,1)}, bf16[2,64,64]{1,2,0:T(8,128)(2,1)}, u32[]{:S(2)}, u32[]{:S(2)}) collective-permute-start(bf16[2,64,64]{1,2,0:T(8,128)(2,1)} %fusion.132), channel_id=1, source_target_pairs={{1,0},{2,1},{3,2},{4,3},{5,4},{6,5},{7,6},{8,7},{9,8},{10,9},{11,1... | collective-permute-start | bytes 49160 | tf_op jit(solution)/shard_map/ppermute | solution.py:16
  33.5 72.1 %collective-permute-start.6 = (bf16[4,64,64]{1,2,0:T(8,128)(2,1)S(1)}, bf16[4,64,64]{1,2,0:T(8,128)(2,1)}, u32[]{:S(2)}, u32[]{:S(2)}) collective-permute-start(bf16[4,64,64]{1,2,0:T(8,128)(2,1)S(1)} %fusion.118), channel_id=1, source_target_pairs={{0,1},{1,2},{2,3},{3,4},{4,5},{5,6},{6,7},{7,8},{8,9},{9,10},{10,1... | collective-permute-start | bytes 98312 | tf_op jit(solution)/shard_map/ppermute | solution.py:15
  77.5 30.0 %collective-permute-start.7 = (bf16[4,64,64]{1,2,0:T(8,128)(2,1)S(1)}, bf16[4,64,64]{1,2,0:T(8,128)(2,1)S(1)}, u32[]{:S(2)}, u32[]{:S(2)}) collective-permute-start(bf16[4,64,64]{1,2,0:T(8,128)(2,1)S(1)} %fusion.118), channel_id=1, source_target_pairs={{1,0},{2,1},{3,2},{4,3},{5,4},{6,5},{7,6},{8,7},{9,8},{10,9},{11,1... | collective-permute-start | bytes 98312 | tf_op jit(solution)/shard_map/ppermute | solution.py:16
  79.6 42.3 %collective-permute-start.4 = (bf16[8,64,64]{1,2,0:T(8,128)(2,1)S(1)}, bf16[8,64,64]{1,2,0:T(8,128)(2,1)S(1)}, u32[]{:S(2)}, u32[]{:S(2)}) collective-permute-start(bf16[8,64,64]{1,2,0:T(8,128)(2,1)S(1)} %fusion.105), channel_id=1, source_target_pairs={{0,1},{1,2},{2,3},{3,4},{4,5},{5,6},{6,7},{7,8},{8,9},{9,10},{10,1... | collective-permute-start | bytes 196616 | tf_op jit(solution)/shard_map/ppermute | solution.py:15
  91.1 32.9 %collective-permute-start.5 = (bf16[8,64,64]{1,2,0:T(8,128)(2,1)S(1)}, bf16[8,64,64]{1,2,0:T(8,128)(2,1)}, u32[]{:S(2)}, u32[]{:S(2)}) collective-permute-start(bf16[8,64,64]{1,2,0:T(8,128)(2,1)S(1)} %fusion.105), channel_id=1, source_target_pairs={{1,0},{2,1},{3,2},{4,3},{5,4},{6,5},{7,6},{8,7},{9,8},{10,9},{11,1... | collective-permute-start | bytes 196616 | tf_op jit(solution)/shard_map/ppermute | solution.py:16
  93.1 37.9 %collective-permute-start.2 = (bf16[16,64,64]{1,2,0:T(8,128)(2,1)S(1)}, bf16[16,64,64]{1,2,0:T(8,128)(2,1)S(1)}, u32[]{:S(2)}, u32[]{:S(2)}) collective-permute-start(bf16[16,64,64]{1,2,0:T(8,128)(2,1)S(1)} %fusion.92), channel_id=1, source_target_pairs={{0,1},{1,2},{2,3},{3,4},{4,5},{5,6},{6,7},{7,8},{8,9},{9,10},{10,1... | collective-permute-start | bytes 393224 | tf_op jit(solution)/shard_map/ppermute | solution.py:15
  105.6 26.0 %collective-permute-start.3 = (bf16[16,64,64]{1,2,0:T(8,128)(2,1)S(1)}, bf16[16,64,64]{1,2,0:T(8,128)(2,1)}, u32[]{:S(2)}, u32[]{:S(2)}) collective-permute-start(bf16[16,64,64]{1,2,0:T(8,128)(2,1)S(1)} %fusion.92), channel_id=1, source_target_pairs={{1,0},{2,1},{3,2},{4,3},{5,4},{6,5},{7,6},{8,7},{9,8},{10,9},{11,1... | collective-permute-start | bytes 393224 | tf_op jit(solution)/shard_map/ppermute | solution.py:16
  107.5 28.3 %collective-permute-start = (bf16[32,64,64]{2,1,0:T(8,128)(2,1)}, bf16[32,64,64]{2,1,0:T(8,128)(2,1)}, u32[]{:S(2)}, u32[]{:S(2)}) collective-permute-start(bf16[32,64,64]{2,1,0:T(8,128)(2,1)} %param.10), channel_id=1, source_target_pairs={{0,1},{1,2},{2,3},{3,4},{4,5},{5,6},{6,7},{7,8},{8,9},{9,10},{10,1... | collective-permute-start | bytes 786440 | tf_op jit(solution)/shard_map/ppermute | solution.py:15
  121.9 24.3 %collective-permute-start.1 = (bf16[32,64,64]{2,1,0:T(8,128)(2,1)}, bf16[32,64,64]{2,1,0:T(8,128)(2,1)}, u32[]{:S(2)}, u32[]{:S(2)}) collective-permute-start(bf16[32,64,64]{2,1,0:T(8,128)(2,1)} %param.10), channel_id=1, source_target_pairs={{1,0},{2,1},{3,2},{4,3},{5,4},{6,5},{7,6},{8,7},{9,8},{10,9},{11,1... | collective-permute-start | bytes 786440 | tf_op jit(solution)/shard_map/ppermute | solution.py:16
  130.9 0.7 copy-start.8
  161.3 12.0 %copy-start.11 = (s32[1024]{0:T(1024)S(1)}, s32[1024]{0:T(1024)}, u32[]{:S(2)}) copy-start(s32[1024]{0:T(1024)} %pad_clamp_fusion) | copy-start | bytes 12292
  173.3 8.0 %copy-start.15 = (bf16[7,16]{1,0:T(8,128)(2,1)S(1)}, bf16[7,16]{1,0:T(8,128)(2,1)}, u32[]{:S(2)}) copy-start(bf16[7,16]{1,0:T(8,128)(2,1)} %fusion.154) | copy-start | bytes 676
  177.4 6.6 %copy-start.4 = (bf16[1,63,64,64]{3,2,1,0:T(8,128)(2,1)S(1)}, bf16[1,63,64,64]{3,2,1,0:T(8,128)(2,1)}, u32[]{:S(2)}) copy-start(bf16[1,63,64,64]{3,2,1,0:T(8,128)(2,1)} %param.11) | copy-start | bytes 1548292
  177.4 6.7 %copy-start.10 = (f32[2,64,64]{2,1,0:T(8,128)S(1)}, f32[2,64,64]{2,1,0:T(8,128)}, u32[]{:S(2)}) copy-start(f32[2,64,64]{2,1,0:T(8,128)} %convolution_bitcast_fusion.5) | copy-start | bytes 98308
  177.4 7.0 %copy-start.7 = (f32[8,64,64]{2,1,0:T(8,128)S(1)}, f32[8,64,64]{2,1,0:T(8,128)}, u32[]{:S(2)}) copy-start(f32[8,64,64]{2,1,0:T(8,128)} %fusion.57) | copy-start | bytes 393220
  181.3 3.0 %copy-start.9 = (f32[4,64,64]{2,1,0:T(8,128)S(1)}, f32[4,64,64]{2,1,0:T(8,128)}, u32[]{:S(2)}) copy-start(f32[4,64,64]{2,1,0:T(8,128)} %convolution_bitcast_fusion.1) | copy-start | bytes 196612
  181.3 3.6 %copy-start.2 = (bf16[256,64,64]{1,2,0:T(8,128)(2,1)S(1)}, bf16[256,64,64]{1,2,0:T(8,128)(2,1)}, u32[]{:S(2)}) copy-start(bf16[256,64,64]{1,2,0:T(8,128)(2,1)} %gather_fusion.1) | copy-start | bytes 6291460
  181.3 3.6 %copy-start.13 = (bf16[16,16]{1,0:T(8,128)(2,1)S(1)}, bf16[16,16]{1,0:T(8,128)(2,1)}, u32[]{:S(2)}) copy-start(bf16[16,16]{1,0:T(8,128)(2,1)} %fusion.152) | copy-start | bytes 1540
  184.7 4.3 %slice-start = ((s8[8388608]{0:T(1024)(128)(4,1)}), s8[4194304]{0:T(1024)(128)(4,1)S(1)}, s32[]{:S(2)}) async-start(s8[8388608]{0:T(1024)(128)(4,1)} %bitcast.318), calls=%async_computation.1 | async-start | bytes 8388608
  184.9 4.5 %slice-start.1 = ((s8[8388608]{0:T(1024)(128)(4,1)}), s8[4194304]{0:T(1024)(128)(4,1)S(1)}, s32[]{:S(2)}) async-start(s8[8388608]{0:T(1024)(128)(4,1)} %bitcast.318), calls=%async_computation.2 | async-start | bytes 8388608
  185.0 4.5 %copy-start.12 = (bf16[32,16]{1,0:T(8,128)(2,1)S(1)}, bf16[32,16]{1,0:T(8,128)(2,1)}, u32[]{:S(2)}) copy-start(bf16[32,16]{1,0:T(8,128)(2,1)} %fusion.151) | copy-start | bytes 3076
  189.5 6.1 %copy-start.1 = (bf16[1,7,16,64,64]{4,3,2,1,0:T(8,128)(2,1)S(1)}, bf16[1,7,16,64,64]{4,3,2,1,0:T(8,128)(2,1)}, u32[]{:S(2)}) copy-start(bf16[1,7,16,64,64]{4,3,2,1,0:T(8,128)(2,1)} %param.16) | copy-start | bytes 2752516
Sparse Core Ops, SparseCore 0:
  67.7 79.0 all-gather.3
where the time goes:
time: 204 us; the launch traced here: 202 us
  starting transfers between devices  61.9 us (30%)
  local copies, waits for them, and re-layouts  53.2 us (26%)
  matrix products  25.8 us (13%)
  blocking collectives  22.9 us (11%)
  other arithmetic  14.2 us (7%)
  between operations  14 us (7%)
  waiting for transfers between devices  10.3 us (5%)
    ppermute x6, starting transfers between devices, with_halo(): before = lax.ppermute(last, axis, up)  50.1 us
    gather x9, local copies, waits for them, and re-layouts, couple_level(): chosen = source[where_from]  41.5 us
    dot_general x7, matrix products, couple_level(): jnp.einsum('ikab,ikbq->iaq', blocks, chosen, preferred_element_type=jnp.f...  20.7 us
    all_gather x1, blocking collectives, on_device(): lax.all_gather(transfer[0:1], 'sub', axis=0, tiled=True)  13.1 us
    ppermute x6, starting transfers between devices, with_halo(): after = lax.ppermute(first, axis, down)  11.9 us
    ppermute x6, waiting for transfers between devices, with_halo(): after = lax.ppermute(first, axis, down)  10.3 us
    all_gather x1, blocking collectives, on_device(): lax.all_gather(coeffs[1], 'sub', axis=0, tiled=True)  9.86 us
    concatenate x6, other arithmetic, with_halo(): array = jnp.concatenate([before, array, after], axis=dim)  6.36 us
  transfers between devices with their start and end apart: 13, of which 1 were waited for; matrix products, arithmetic and copies ran while one was open for 30% of the time, Pallas kernels for 0%

commit v1 on v0

v1 whole, which is shorter than its diff:
```python
import jax
import jax.numpy as jnp
from jax import lax
from jax.experimental import pallas as pl
from jax.experimental.pallas import tpu as pltpu
from jax.sharding import PartitionSpec as P

F32 = jnp.float32
BF16 = jnp.bfloat16
MESH = pl.DeviceIdType.MESH

R = 64
K = 16
C = 32
UP = C - 1
SLOTS = 2 * C - 1
LEAF = 32
SUB = 8
NZ, NY = 8, 4
DEVICES = LEAF * SUB
ZERO_B = 3 * C
ZERO_U = 3 * UP
ZERO_P = LEAF * 8
NT = (((1,), (1,)), ((), ()))


def mm(a, b):
    return jnp.dot(a, b, preferred_element_type=F32)


def mm_nt(a, b):
    return lax.dot_general(a, b, NT, preferred_element_type=F32)


def fold(block):
    return jnp.concatenate([block[: R // 2], block[R // 2 :]], axis=1)


def couple(index, first, slot, blocks, source):
    total = jnp.zeros((R, R), F32)
    for k0 in range(0, K, 4):
        left = jnp.concatenate([blocks[slot, k] for k in range(k0, k0 + 4)], axis=1)
        right = jnp.concatenate([source[index[k, slot]] for k in range(k0, k0 + 4)], axis=0)
        total = total + mm(left, right)
    return total


def kernel(
    bottom, transfer, coarse_transfer, coupling, coarse_coupling, partners, counts, coarse_partners, coarse_counts,
    out,
    xb, xu, f, cf, s, cs, cscat, ft, g, w, zb, zu,
    send_b, send_u, recv_b, recv_u, pt, r, mine, pool, poolf, ys, yr, outv,
    part_v, count_v, index_v, index_s, cpart_s, ccount_s, cindex_s,
    load_sem, small_sem, out_sem, halo_s, halo_r, lift_s, lift_r, z_s, z_r, y_s, y_r, low_s, low_r,
):
    leaf = lax.axis_index("leaf")
    sub = lax.axis_index("sub")
    me = leaf * SUB + sub
    at_z = lax.div(leaf, NY)
    at_y = lax.rem(leaf, NY)
    after = lax.rem(me + 1, DEVICES)
    before = lax.rem(me + DEVICES - 1, DEVICES)
    sides = [(lax.div(d, SUB), lax.rem(d, SUB)) for d in (before, after)]
    group = [lax.rem(sub + i, SUB) for i in range(1, SUB)]
    along_z = [lax.rem(at_z + i, NZ) * NY + at_y for i in range(1, NZ)]
    along_y = [at_z * NY + lax.rem(at_y + i, NY) for i in range(1, NY)]

    load = lambda a, b, i: pltpu.make_async_copy(a, b, load_sem.at[i])
    get_x = load(bottom, xb.at[pl.ds(C, C)], 0)
    get_fb = load(transfer.at[pl.ds(UP, C)], f.at[pl.ds(UP, C)], 1)
    get_fu = load(transfer.at[pl.ds(0, UP)], f.at[pl.ds(0, UP)], 2)
    get_cf = load(coarse_transfer, cf, 3)
    get_cs = load(coarse_coupling, cs, 4)
    get_su = load(coupling.at[pl.ds(0, UP)], s.at[pl.ds(0, UP)], 5)
    get_sb = load(coupling.at[pl.ds(UP, C)], s.at[pl.ds(UP, C)], 6)
    small = lambda a, b, i: pltpu.make_async_copy(a, b, small_sem.at[i])
    get_part = small(partners, part_v, 0)
    get_count = small(counts, count_v, 1)
    get_cpart = small(coarse_partners, cpart_s, 2)
    get_ccount = small(coarse_counts, ccount_s, 3)
    for copy in (get_x, get_fb, get_fu, get_part, get_count, get_cf, get_cpart, get_ccount):
        copy.start()

    barrier = pltpu.get_barrier_semaphore()
    for peer in sides:
        pl.semaphore_signal(barrier, inc=1, device_id=peer, device_id_type=MESH)
    for peer in group:
        pl.semaphore_signal(barrier, inc=1, device_id=(leaf, peer), device_id_type=MESH)
    for peer in along_z + along_y:
        pl.semaphore_signal(barrier, inc=1, device_id=(peer, sub), device_id_type=MESH)

    xb[ZERO_B] = jnp.zeros((R, R), BF16)
    xu[ZERO_U] = jnp.zeros((R, R), BF16)
    poolf[ZERO_P] = jnp.zeros((8, R), F32)

    get_x.wait()
    for i in range(C):
        send_b[i] = fold(xb[C + i])
    get_su.start()
    pl.semaphore_wait(barrier, 2 + (SUB - 1) + (NZ - 1) + (NY - 1))

    def remote(src, dst, ss, rs, peer):
        return pltpu.make_async_remote_copy(
            src_ref=src, dst_ref=dst, send_sem=ss, recv_sem=rs, device_id=peer, device_id_type=MESH
        )

    halo_b = [remote(send_b, recv_b.at[1 - i], halo_s.at[i], halo_r.at[i], sides[i]) for i in range(2)]
    halo_u = [remote(send_u, recv_u.at[1 - i], halo_s.at[2 + i], halo_r.at[2 + i], sides[i]) for i in range(2)]
    for copy in halo_b:
        copy.start()

    get_fb.wait()
    get_fu.wait()
    n = C // 2
    while n >= 1:
        for i in range(n):
            a = 2 * (n + i) - 1
            left = jnp.concatenate([f[a], f[a + 1]], axis=1)
            right = (xb[pl.ds(C + 2 * i, 2)] if n == C // 2 else xu[pl.ds(UP + a, 2)]).reshape(2 * R, R)
            xu[UP + n + i - 1] = mm(left, right).astype(BF16)
        n //= 2
    lifted = jnp.transpose(mm(f[0], xu[UP]))
    pt[...] = lifted.reshape(SUB, 8, R)
    lifts = [
        remote(pt.at[peer], r.at[sub], lift_s.at[i], lift_r.at[i], (leaf, peer)) for i, peer in enumerate(group)
    ]
    for copy in lifts:
        copy.start()
    r[pl.ds(sub, 1)] = pt[pl.ds(sub, 1)]

    for i in range(UP):
        send_u[i] = fold(xu[UP + i])
    for copy in halo_u:
        copy.start()
    get_sb.start()
    get_cs.start()

    get_part.wait()
    get_count.wait()
    node = lax.broadcasted_iota(jnp.int32, (K, SLOTS), 1) + 1
    step = lax.broadcasted_iota(jnp.int32, (K, SLOTS), 0)
    width = jnp.ones((K, SLOTS), jnp.int32)
    for t in range(1, 6):
        width = jnp.where(node >= 2**t, 2**t, width)
    target = node - width + part_v[...]
    window = jnp.where(target < 0, 0, jnp.where(target < width, 1, 2))
    where_u = window * UP + (width - 1) + target + width - window * width
    is_bottom = node >= C
    where_from = jnp.where(is_bottom, C + target, where_u)
    ended = step >= jnp.broadcast_to(count_v[...], (K, SLOTS))
    where_from = jnp.where(ended, jnp.where(is_bottom, ZERO_B, ZERO_U), where_from)
    index_v[:, pl.ds(0, SLOTS)] = where_from
    to_smem = small(index_v, index_s, 4)
    to_smem.start()

    g[0] = jnp.transpose(f[0])
    for h in range(1, C):
        ft[h - 1] = jnp.transpose(jnp.concatenate([f[2 * h - 1], f[2 * h]], axis=1))
    for h in range(1, C):
        g[pl.ds(2 * h - 1, 2)] = mm(ft[h - 1], g[h - 1]).astype(BF16).reshape(2, R, R)

    get_cf.wait()
    for copy in lifts:
        copy.wait_recv()
    rounded = lambda a: a.astype(BF16).astype(F32)
    x2 = [rounded(r[2 * j] + r[2 * j + 1]) for j in range(4)]
    pair_a = jnp.concatenate([x2[0], x2[1]], axis=1)
    pair_b = jnp.concatenate([x2[2], x2[3]], axis=1)
    none = jnp.zeros((8, 2 * R), F32)
    left = jnp.concatenate(
        [jnp.concatenate([pair_a, none], axis=1), jnp.concatenate([none, pair_b], axis=1)], axis=0
    ).astype(BF16)
    x1 = rounded(mm_nt(left, jnp.concatenate([cf[2 + j] for j in range(4)], axis=1)))
    pair_c = jnp.concatenate([x1[:8], x1[8:]], axis=1)
    x0 = mm_nt(pair_c.astype(BF16), jnp.concatenate([cf[0], cf[1]], axis=1))
    pair_d = jnp.concatenate([x0, jnp.zeros((8, R), F32)], axis=1)
    mine[...] = jnp.concatenate([pair_a, pair_b, pair_c, pair_d], axis=0).astype(BF16)
    over_z = [
        remote(mine, pool.at[at_y, at_z], z_s.at[i], z_r.at[i], (peer, sub)) for i, peer in enumerate(along_z)
    ]
    for copy in over_z:
        copy.start()
    pool[pl.ds(at_y, 1), pl.ds(at_z, 1)] = mine[...].reshape(1, 1, 32, 2 * R)

    get_cpart.wait()
    get_ccount.wait()
    for t in range(3):
        for j in range(2**t):
            i = 2**t - 1 + j
            for k in range(K):
                p = cpart_s[i, 0, k]
                its = lax.shift_right_logical(p, t)
                inside = p - lax.shift_left(its, t)
                place = lax.rem(its, NY) * NZ + lax.div(its, NY)
                place = place * 8 + (0, 4, 6)[2 - t] + inside
                cindex_s[i * K + k] = jnp.where(k < ccount_s[0, i], place, ZERO_P)
    get_cs.wait()
    for i in range(7):
        for k0 in range(0, K, 4):
            cscat[i, :, pl.ds(k0 * R, 4 * R)] = jnp.concatenate([cs[i, k] for k in range(k0, k0 + 4)], axis=1)

    for copy in over_z:
        copy.wait_recv()
    over_y = [
        remote(pool.at[at_y], pool.at[at_y], y_s.at[i], y_r.at[i], (peer, sub)) for i, peer in enumerate(along_y)
    ]
    for copy in over_y:
        copy.start()

    for copy in halo_b + halo_u:
        copy.wait_recv()
    to_smem.wait()
    for side in range(2):
        for i in range(UP):
            v = recv_u[side, i]
            xu[2 * UP * side + i] = jnp.concatenate([v[:, :R], v[:, R:]], axis=0)
        for i in range(C):
            v = recv_b[side, i]
            xb[2 * C * side + i] = jnp.concatenate([v[:, :R], v[:, R:]], axis=0)
    for side, end in ((0, 0), (1, DEVICES - 1)):

        @pl.when(me == end)
        def _():
            xu[pl.ds(2 * UP * side, UP)] = jnp.zeros((UP, R, R), BF16)
            xb[pl.ds(2 * C * side, C)] = jnp.zeros((C, R, R), BF16)

    get_su.wait()

    @pl.loop(0, UP, unroll=UP)
    def _(i):
        zu[i] = couple(index_s, 0, i, s, xu)

    w[0] = zu[0].astype(BF16)
    for h in range(1, C // 2):
        low = zu[pl.ds(2 * h - 1, 2)].reshape(2 * R, R) + mm(ft[h - 1], w[h - 1])
        w[pl.ds(2 * h - 1, 2)] = low.astype(BF16).reshape(2, R, R)

    for copy in over_y:
        copy.wait_recv()
    for y in range(NY):
        for z in range(NZ):
            v = pool[y, z].astype(F32)
            for b in range(4):
                poolf[(y * NZ + z) * 8 + 2 * b] = v[8 * b : 8 * b + 8, :R]
                poolf[(y * NZ + z) * 8 + 2 * b + 1] = v[8 * b : 8 * b + 8, R:]
    zc = []
    for i in range(7):
        left = jnp.concatenate([poolf[cindex_s[i * K + k]] for k in range(K)], axis=1)
        zc.append(mm_nt(left.astype(BF16), cscat[i]))
    y1 = jnp.concatenate([zc[1], zc[2]], axis=1) + mm(
        zc[0].astype(BF16), jnp.concatenate([cf[0], cf[1]], axis=1)
    )
    y1 = y1.astype(BF16)
    y2a = jnp.concatenate([zc[3], zc[4]], axis=1) + mm(y1[:, :R], jnp.concatenate([cf[2], cf[3]], axis=1))
    y2b = jnp.concatenate([zc[5], zc[6]], axis=1) + mm(y1[:, R:], jnp.concatenate([cf[4], cf[5]], axis=1))
    for j, v in enumerate((y2a, y2b)):
        v = rounded(v)
        ys[2 * j] = v[:, :R]
        ys[2 * j + 1] = v[:, R:]
    lows = [
        remote(ys.at[lax.div(peer, 2)], yr.at[sub], low_s.at[i], low_r.at[i], (leaf, peer))
        for i, peer in enumerate(group)
    ]
    for copy in lows:
        copy.start()
    yr[pl.ds(sub, 1)] = ys[pl.ds(lax.div(sub, 2), 1)]

    get_sb.wait()

    @pl.loop(0, C, unroll=C)
    def _(i):
        zb[i] = couple(index_s, 0, UP + i, s, xb)

    for i in range(C // 2):
        h = C // 2 + i
        low = zb[pl.ds(2 * i, 2)].reshape(2 * R, R) + mm(ft[h - 1], w[h - 1])
        zb[pl.ds(2 * i, 2)] = low.reshape(2, R, R)

    for copy in lows:
        copy.wait_recv()
    yp = yr[...].reshape(R, R).astype(BF16)
    puts = []
    part = C // 4
    for c in range(4):
        far = mm_nt(g[pl.ds(UP + c * part, part)].reshape(part * R, R), yp).reshape(part, R, R)
        outv[pl.ds(c * part, part)] = (zb[pl.ds(c * part, part)] + far).astype(BF16)
        put = pltpu.make_async_copy(
            outv.at[pl.ds(c * part, part)], out.at[pl.ds(c * part, part)], out_sem.at[c]
        )
        put.start()
        puts.append(put)
    for copy in halo_b + halo_u + lifts + over_z + over_y + lows:
        copy.wait_send()
    for put in puts:
        put.wait()


def on_device(
    bottom, transfer, coarse_transfer, coupling, partners, counts, coarse_coupling, coarse_partners, coarse_counts
):
    dma = pltpu.SemaphoreType.DMA
    any_space = pl.BlockSpec(memory_space=pl.ANY)
    return pl.pallas_call(
        kernel,
        out_shape=jax.ShapeDtypeStruct((C, R, R), BF16),
        in_specs=[any_space] * 9,
        out_specs=any_space,
        scratch_shapes=[
            pltpu.VMEM((3 * C + 1, R, R), BF16),
            pltpu.VMEM((3 * UP + 1, R, R), BF16),
            pltpu.VMEM((SLOTS, R, R), BF16),
            pltpu.VMEM((6, R, R), BF16),
            pltpu.VMEM((SLOTS, K, R, R), BF16),
            pltpu.VMEM((7, K, R, R), BF16),
            pltpu.VMEM((7, R, K * R), BF16),
            pltpu.VMEM((UP, 2 * R, R), BF16),
            pltpu.VMEM((SLOTS, R, R), BF16),
            pltpu.VMEM((UP, R, R), BF16),
            pltpu.VMEM((C, R, R), F32),
            pltpu.VMEM((UP, R, R), F32),
            pltpu.VMEM((C, R // 2, 2 * R), BF16),
            pltpu.VMEM((UP, R // 2, 2 * R), BF16),
            pltpu.VMEM((2, C, R // 2, 2 * R), BF16),
            pltpu.VMEM((2, UP, R // 2, 2 * R), BF16),
            pltpu.VMEM((SUB, 8, R), F32),
            pltpu.VMEM((SUB, 8, R), F32),
            pltpu.VMEM((32, 2 * R), BF16),
            pltpu.VMEM((NY, NZ, 32, 2 * R), BF16),
            pltpu.VMEM((LEAF * 8 + 1, 8, R), F32),
            pltpu.VMEM((4, 8, R), F32),
            pltpu.VMEM((SUB, 8, R), F32),
            pltpu.VMEM((C, R, R), BF16),
            pltpu.VMEM((K, SLOTS), jnp.int32),
            pltpu.VMEM((1, SLOTS), jnp.int32),
            pltpu.VMEM((K, 128), jnp.int32),
            pltpu.SMEM((K, 128), jnp.int32),
            pltpu.SMEM((7, 1, K), jnp.int32),
            pltpu.SMEM((1, 7), jnp.int32),
            pltpu.SMEM((7 * K,), jnp.int32),
            dma((7,)), dma((5,)), dma((4,)),
            dma((4,)), dma((4,)), dma((7,)), dma((7,)), dma((7,)), dma((7,)),
            dma((3,)), dma((3,)), dma((7,)), dma((7,)),
        ],
        compiler_params=pltpu.CompilerParams(
            collective_id=0, has_side_effects=True, vmem_limit_bytes=56 * 2**20
        ),
        cost_estimate=pl.CostEstimate(flops=700_000_000, bytes_accessed=21_000_000, transcendentals=0),
    )(
        bottom,
        transfer.reshape(SLOTS, R, R),
        coarse_transfer.reshape(6, R, R),
        coupling.reshape(SLOTS, K, R, R),
        coarse_coupling.reshape(7, K, R, R),
        jnp.transpose(partners, (0, 2, 1)).reshape(K, SLOTS),
        counts,
        jnp.transpose(coarse_partners, (1, 0, 2)),
        coarse_counts,
    )


def solution(mesh):
    wide = P(("leaf", "sub"))
    placed = (wide, wide, P("leaf"), wide, wide, wide, P("leaf"), P("leaf"), P("leaf"))
    return jax.shard_map(on_device, mesh=mesh, in_specs=placed, out_specs=wide, check_vma=False)
```

time: 204 us -> 34.2 us (0.17)
  the two profiles are of different devices: /device:TPU:127 before, /device:TPU:1 now
where the time goes in v1:
time: 34.2 us; the launch traced here: 34 us
  Pallas kernels  32.1 us (94%)
  local copies, waits for them, and re-layouts  1.87 us (5%)
    pallas_call x1, Pallas kernels, on_device(): pl.pallas_call(kernel, out_shape=jax.ShapeDtypeStruct((C, R, R), BF16), i...  32.1 us
    unnamed x1, local copies, waits for them, and re-layouts  1.87 us

profile of v1, /device:TPU:1, one launch (start us, length us, event | category | flops | bytes accessed | tf_op | source)
XLA Modules:
  0.0 34.0 jit_solution(14862760978122878665)
XLA Ops:
  0.0 32.1 %shard_map.91 = bf16[32,64,64]{2,1,0:T(8,128)(2,1)} custom-call(bf16[32,64,64]{2,1,0:T(8,128)(2,1)} %bottom.1, bf16[63,64,64]{2,1,0:T(8,128)(2,1)} %bitcast.10, bf16[6,64,64]{2,1,0:T(8,128)(2,1)} %bitcast.11, bf16[63,16,64,64]{3,2,1,0:T(8,128)(2,1)} %bitcast.8, bf16[7,16,64,64]{3,2,1,0:T(8,128)(2,1)} %bitcast.9, s32[16,63]{1,0:T(8,128)} %bitcast.12, ...), custom_call_target="tpu_custom_call" | custom-call | flops 700000000 | bytes 21000000 | tf_op jit(solution)/shard_map/pallas_call | solution.py:303
  32.1 1.9 %copy.11 = bf16[32,64,64]{2,1,0:T(8,128)(2,1)} copy(bf16[32,64,64]{2,1,0:T(8,128)(2,1)} %shard_map.91) | data formatting | bytes 524288

commit v2 on v1

v2 whole, which is shorter than its diff:
```python
import jax
import jax.numpy as jnp
from jax import lax
from jax.experimental import pallas as pl
from jax.experimental.pallas import tpu as pltpu
from jax.sharding import PartitionSpec as P

F32 = jnp.float32
BF16 = jnp.bfloat16
MESH = pl.DeviceIdType.MESH

R = 64
K = 16
C = 32
UP = C - 1
SLOTS = 2 * C - 1
LEAF = 32
SUB = 8
NZ, NY = 8, 4
DEVICES = LEAF * SUB
ZERO_B = 3 * C
ZERO_U = 3 * UP
ZERO_P = 3 * LEAF
H = R // 2
NT = (((1,), (1,)), ((), ()))


def mm(a, b):
    return jnp.dot(a, b, preferred_element_type=F32)


def mm_nt(a, b):
    return lax.dot_general(a, b, NT, preferred_element_type=F32)


def fold(block):
    half = block.shape[0] // 2
    return jnp.concatenate([block[:half], block[half:]], axis=1)


def unfold(block):
    return jnp.concatenate([block[:, :R], block[:, R:]], axis=0)


def couple(index, first, slot, blocks, source):
    total = jnp.zeros((R, R), F32)
    for k0 in range(0, K, 4):
        left = jnp.concatenate([blocks[slot, k] for k in range(k0, k0 + 4)], axis=1)
        right = jnp.concatenate([source[index[k, slot]] for k in range(k0, k0 + 4)], axis=0)
        total = total + mm(left, right)
    return total


def kernel(
    bottom, transfer, coarse_transfer, coupling, coarse_coupling, partners, counts, coarse_partners, coarse_counts,
    out,
    xb, xu, f, cf, s, cs, cscat, ft, g, w, zb, zu,
    send_b, send_u, recv_b, recv_u, pt, pr, lift, mine, pool, xc, ys, yr,
    part_v, count_v, index_v, index_s, cpart_s, ccount_s, cindex_s,
    load_sem, small_sem, halo_s, halo_r, core_s, core_r, z_s, z_r, y_s, y_r, low_s, low_r,
):
    leaf = lax.axis_index("leaf")
    sub = lax.axis_index("sub")
    me = leaf * SUB + sub
    at_z = lax.div(leaf, NY)
    at_y = lax.rem(leaf, NY)
    chip = lax.div(sub, 2)
    core = lax.rem(sub, 2)
    after = lax.rem(me + 1, DEVICES)
    before = lax.rem(me + DEVICES - 1, DEVICES)
    sides = [(lax.div(d, SUB), lax.rem(d, SUB)) for d in (before, after)]
    group = [lax.rem(sub + i, SUB) for i in range(1, SUB)]
    along_z = [lax.rem(at_z + i, NZ) * NY + at_y for i in range(1, NZ)]
    along_y = [at_z * NY + lax.rem(at_y + i, NY) for i in range(1, NY)]

    load = lambda a, b, i: pltpu.make_async_copy(a, b, load_sem.at[i])
    get_x = load(bottom, xb.at[pl.ds(C, C)], 0)
    get_fb = load(transfer.at[pl.ds(UP, C)], f.at[pl.ds(UP, C)], 1)
    get_fu = load(transfer.at[pl.ds(0, UP)], f.at[pl.ds(0, UP)], 2)
    get_cf = load(coarse_transfer, cf, 3)
    get_cs = load(coarse_coupling, cs, 4)
    get_su = load(coupling.at[pl.ds(0, UP)], s.at[pl.ds(0, UP)], 5)
    get_sb = load(coupling.at[pl.ds(UP, C)], s.at[pl.ds(UP, C)], 6)
    small = lambda a, b, i: pltpu.make_async_copy(a, b, small_sem.at[i])
    get_part = small(partners, part_v, 0)
    get_count = small(counts, count_v, 1)
    get_cpart = small(coarse_partners, cpart_s, 2)
    get_ccount = small(coarse_counts, ccount_s, 3)
    for copy in (get_x, get_fb, get_fu, get_cf):
        copy.start()
    barrier = pltpu.get_barrier_semaphore()
    for peer in along_z + along_y:
        pl.semaphore_signal(barrier, inc=1, device_id=(peer, sub), device_id_type=MESH)
    for peer in sides:
        pl.semaphore_signal(barrier, inc=1, device_id=peer, device_id_type=MESH)
    for peer in group:
        pl.semaphore_signal(barrier, inc=1, device_id=(leaf, peer), device_id_type=MESH)

    for copy in (get_part, get_count, get_cpart, get_ccount):
        copy.start()
    xb[ZERO_B] = jnp.zeros((R, R), BF16)
    xu[ZERO_U] = jnp.zeros((R, R), BF16)
    xc[ZERO_P] = jnp.zeros((H, R), BF16)

    get_x.wait()
    get_fb.wait()
    get_fu.wait()
    n = C // 2
    while n >= 1:
        for i in range(n):
            a = 2 * (n + i) - 1
            left = jnp.concatenate([f[a], f[a + 1]], axis=1)
            right = (xb[pl.ds(C + 2 * i, 2)] if n == C // 2 else xu[pl.ds(UP + a, 2)]).reshape(2 * R, R)
            xu[UP + n + i - 1] = mm(left, right).astype(BF16)
        n //= 2
    pt[...] = jnp.transpose(mm(f[0], xu[UP])).reshape(2, H, R)

    get_cf.wait()
    ones = lax.broadcasted_iota(jnp.int32, (R, R), 0) == lax.broadcasted_iota(jnp.int32, (R, R), 1)
    lift[pl.ds(0, R)] = ones.astype(F32).astype(BF16)
    lift[pl.ds(R, R)] = cf[2 + chip]
    lift[pl.ds(2 * R, R)] = mm(cf[lax.div(chip, 2)], cf[2 + chip]).astype(BF16)
    for i in range(C):
        send_b[i] = fold(xb[C + i])

    pl.semaphore_wait(barrier, 2 + (SUB - 1) + (NZ - 1) + (NY - 1))

    def remote(src, dst, ss, rs, peer):
        return pltpu.make_async_remote_copy(
            src_ref=src, dst_ref=dst, send_sem=ss, recv_sem=rs, device_id=peer, device_id_type=MESH
        )

    swap = remote(pt.at[1 - core], pr, core_s.at[0], core_r.at[0], (leaf, chip * 2 + 1 - core))
    swap.start()
    get_cs.start()

    halo_b = [remote(send_b, recv_b.at[1 - i], halo_s.at[i], halo_r.at[i], sides[i]) for i in range(2)]
    halo_u = [remote(send_u, recv_u.at[1 - i], halo_s.at[2 + i], halo_r.at[2 + i], sides[i]) for i in range(2)]
    for copy in halo_b:
        copy.start()

    swap.wait_recv()
    node = (pt[pl.ds(core, 1)].reshape(H, R) + pr[...]).astype(BF16)
    piece = mm_nt(node, lift[...])
    mine[pl.ds(0, H)] = piece[:, : 2 * R].astype(BF16)
    mine[pl.ds(H, H // 2)] = fold(piece[:, 2 * R :]).astype(BF16)
    over_z = [
        remote(mine, pool.at[at_y, at_z], z_s.at[i], z_r.at[i], (peer, sub)) for i, peer in enumerate(along_z)
    ]
    over_y = [
        [
            remote(
                mine if i == NZ - 1 else pool.at[at_y, from_z],
                pool.at[at_y, from_z],
                y_s.at[i, m],
                y_r.at[i, m],
                (peer, sub),
            )
            for m, peer in ((1, along_y[1]), (0, along_y[0]), (2, along_y[2]))
        ]
        for i, from_z in enumerate([lax.rem(at_z + NZ - 1 - i, NZ) for i in range(NZ)])
    ]
    for i in (0, 6, 1, 5, 2, 4, 3):
        over_z[i].start()
    for copy in over_y[NZ - 1]:
        copy.start()
    get_sb.start()
    pool[pl.ds(at_y, 1), pl.ds(at_z, 1)] = mine[...].reshape(1, 1, 3 * H // 2, 2 * R)

    for i in range(UP):
        send_u[i] = fold(xu[UP + i])
    for copy in halo_u:
        copy.start()

    get_part.wait()
    get_count.wait()
    node = lax.broadcasted_iota(jnp.int32, (K, SLOTS), 1) + 1
    step = lax.broadcasted_iota(jnp.int32, (K, SLOTS), 0)
    width = jnp.ones((K, SLOTS), jnp.int32)
    for t in range(1, 6):
        width = jnp.where(node >= 2**t, 2**t, width)
    target = node - width + part_v[...]
    window = jnp.where(target < 0, 0, jnp.where(target < width, 1, 2))
    where_u = window * UP + (width - 1) + target + width - window * width
    is_bottom = node >= C
    where_from = jnp.where(is_bottom, C + target, where_u)
    ended = step >= jnp.broadcast_to(count_v[...], (K, SLOTS))
    where_from = jnp.where(ended, jnp.where(is_bottom, ZERO_B, ZERO_U), where_from)
    index_v[:, pl.ds(0, SLOTS)] = where_from
    to_smem = small(index_v, index_s, 4)
    to_smem.start()

    g[0] = jnp.transpose(f[0])
    for h in range(1, C):
        ft[h - 1] = jnp.transpose(jnp.concatenate([f[2 * h - 1], f[2 * h]], axis=1))
    for h in range(1, C):
        g[pl.ds(2 * h - 1, 2)] = mm(ft[h - 1], g[h - 1]).astype(BF16).reshape(2, R, R)

    get_cpart.wait()
    get_ccount.wait()
    for t in range(3):
        for j in range(2**t):
            i = 2**t - 1 + j
            for k in range(K):
                p = cpart_s[i, 0, k]
                its = lax.shift_right_logical(p, t)
                inside = p - lax.shift_left(its, t)
                place = lax.rem(its, NY) * NZ + lax.div(its, NY)
                here = jnp.logical_and(k < ccount_s[0, i], inside == lax.div(chip, 2 ** (2 - t)))
                cindex_s[i * K + k] = jnp.where(here, place + (2 - t) * LEAF, ZERO_P)
    get_cs.wait()
    for i in range(7):
        for k0 in range(0, K, 4):
            cscat[i, :, pl.ds(k0 * R, 4 * R)] = jnp.concatenate([cs[i, k] for k in range(k0, k0 + 4)], axis=1)

    for i in (0, 6, 1, 5, 2, 4, 3):
        over_z[i].wait_recv()
        for copy in over_y[i]:
            copy.start()
    get_su.start()

    for copy in halo_b:
        copy.wait_recv()
    to_smem.wait()
    for side in range(2):
        for i in range(C):
            xb[2 * C * side + i] = unfold(recv_b[side, i])
    for side, end in ((0, 0), (1, DEVICES - 1)):

        @pl.when(me == end)
        def _():
            xb[pl.ds(2 * C * side, C)] = jnp.zeros((C, R, R), BF16)

    get_sb.wait()

    @pl.loop(0, C, unroll=C)
    def _(i):
        zb[i] = couple(index_s, 0, UP + i, s, xb)

    def spread(y, z):
        at = y * NZ + z
        v = pool[y, z]
        xc[at] = v[:H, :R]
        xc[LEAF + at] = v[:H, R:]
        xc[2 * LEAF + at] = unfold(v[H:])

    for i in range(NZ):
        spread(at_y, lax.rem(at_z + i, NZ))
    for i in (7, 0, 6, 1, 5, 2, 4, 3):
        for copy in over_y[i]:
            copy.wait_recv()
        for m in range(1, NY):
            spread(lax.rem(at_y + m, NY), lax.rem(at_z + NZ - 1 - i, NZ))
    zc = []
    for i in range(7):
        left = jnp.concatenate([xc[cindex_s[i * K + k]] for k in range(K)], axis=1)
        zc.append(mm_nt(left, cscat[i]))
    y1 = jnp.concatenate([zc[1], zc[2]], axis=1) + mm(
        zc[0].astype(BF16), jnp.concatenate([cf[0], cf[1]], axis=1)
    )
    y1 = y1.astype(BF16)
    y2a = jnp.concatenate([zc[3], zc[4]], axis=1) + mm(y1[:, :R], jnp.concatenate([cf[2], cf[3]], axis=1))
    y2b = jnp.concatenate([zc[5], zc[6]], axis=1) + mm(y1[:, R:], jnp.concatenate([cf[4], cf[5]], axis=1))
    for j, v in enumerate((y2a, y2b)):
        ys[2 * j] = fold(v[:, :R])
        ys[2 * j + 1] = fold(v[:, R:])
    lows = [
        remote(ys.at[lax.div(peer, 2)], yr.at[sub], low_s.at[i], low_r.at[i], (leaf, peer))
        for i, peer in enumerate(group)
    ]
    for copy in lows:
        copy.start()
    yr[pl.ds(sub, 1)] = ys[pl.ds(lax.div(sub, 2), 1)]

    for copy in halo_u:
        copy.wait_recv()
    for side in range(2):
        for i in range(UP):
            xu[2 * UP * side + i] = unfold(recv_u[side, i])
    for side, end in ((0, 0), (1, DEVICES - 1)):

        @pl.when(me == end)
        def _():
            xu[pl.ds(2 * UP * side, UP)] = jnp.zeros((UP, R, R), BF16)

    get_su.wait()

    @pl.loop(0, UP, unroll=UP)
    def _(i):
        zu[i] = couple(index_s, 0, i, s, xu)

    w[0] = zu[0].astype(BF16)
    for h in range(1, C // 2):
        low = zu[pl.ds(2 * h - 1, 2)].reshape(2 * R, R) + mm(ft[h - 1], w[h - 1])
        w[pl.ds(2 * h - 1, 2)] = low.astype(BF16).reshape(2, R, R)

    for i in range(C // 2):
        h = C // 2 + i
        low = zb[pl.ds(2 * i, 2)].reshape(2 * R, R) + mm(ft[h - 1], w[h - 1])
        zb[pl.ds(2 * i, 2)] = low.reshape(2, R, R)

    for copy in lows:
        copy.wait_recv()
    halves = [unfold((yr[c] + yr[2 + c]) + (yr[4 + c] + yr[6 + c])) for c in range(2)]
    yp = jnp.concatenate(halves, axis=0).astype(BF16)
    far = mm_nt(g[pl.ds(UP, C)].reshape(C * R, R), yp).reshape(C, R, R)
    out[...] = (zb[...] + far).astype(BF16)
    for copy in [swap] + halo_b + halo_u + over_z + sum(over_y, []) + lows:
        copy.wait_send()


def on_device(
    bottom, transfer, coarse_transfer, coupling, partners, counts, coarse_coupling, coarse_partners, coarse_counts
):
    dma = pltpu.SemaphoreType.DMA
    any_space = pl.BlockSpec(memory_space=pltpu.HBM)
    return pl.pallas_call(
        kernel,
        out_shape=pltpu.VMEM((C, R, R), BF16),
        in_specs=[any_space] * 9,
        out_specs=pl.BlockSpec(memory_space=pltpu.VMEM),
        scratch_shapes=[
            pltpu.VMEM((3 * C + 1, R, R), BF16),
            pltpu.VMEM((3 * UP + 1, R, R), BF16),
            pltpu.VMEM((SLOTS, R, R), BF16),
            pltpu.VMEM((6, R, R), BF16),
            pltpu.VMEM((SLOTS, K, R, R), BF16),
            pltpu.VMEM((7, K, R, R), BF16),
            pltpu.VMEM((7, R, K * R), BF16),
            pltpu.VMEM((UP, 2 * R, R), BF16),
            pltpu.VMEM((SLOTS, R, R), BF16),
            pltpu.VMEM((UP, R, R), BF16),
            pltpu.VMEM((C, R, R), F32),
            pltpu.VMEM((UP, R, R), F32),
            pltpu.VMEM((C, R // 2, 2 * R), BF16),
            pltpu.VMEM((UP, R // 2, 2 * R), BF16),
            pltpu.VMEM((2, C, R // 2, 2 * R), BF16),
            pltpu.VMEM((2, UP, R // 2, 2 * R), BF16),
            pltpu.VMEM((2, H, R), F32),
            pltpu.VMEM((H, R), F32),
            pltpu.VMEM((3 * R, R), BF16),
            pltpu.VMEM((3 * H // 2, 2 * R), BF16),
            pltpu.VMEM((NY, NZ, 3 * H // 2, 2 * R), BF16),
            pltpu.VMEM((3 * LEAF + 1, H, R), BF16),
            pltpu.VMEM((4, H // 2, 2 * R), F32),
            pltpu.VMEM((SUB, H // 2, 2 * R), F32),
            pltpu.VMEM((K, SLOTS), jnp.int32),
            pltpu.VMEM((1, SLOTS), jnp.int32),
            pltpu.VMEM((K, 128), jnp.int32),
            pltpu.SMEM((K, 128), jnp.int32),
            pltpu.SMEM((7, 1, K), jnp.int32),
            pltpu.SMEM((1, 7), jnp.int32),
            pltpu.SMEM((7 * K,), jnp.int32),
            dma((7,)), dma((5,)),
            dma((4,)), dma((4,)), dma((1,)), dma((1,)), dma((7,)), dma((7,)),
            dma((NZ, NY - 1)), dma((NZ, NY - 1)), dma((7,)), dma((7,)),
        ],
        compiler_params=pltpu.CompilerParams(
            collective_id=0, has_side_effects=True, vmem_limit_bytes=64_800 * 2**10
        ),
        cost_estimate=pl.CostEstimate(flops=700_000_000, bytes_accessed=21_000_000, transcendentals=0),
    )(
        bottom,
        transfer.reshape(SLOTS, R, R),
        coarse_transfer.reshape(6, R, R),
        coupling.reshape(SLOTS, K, R, R),
        coarse_coupling.reshape(7, K, R, R),
        jnp.transpose(partners, (0, 2, 1)).reshape(K, SLOTS),
        counts,
        jnp.transpose(coarse_partners, (1, 0, 2)),
        coarse_counts,
    )


def solution(mesh):
    wide = P(("leaf", "sub"))
    placed = (wide, wide, P("leaf"), wide, wide, wide, P("leaf"), P("leaf"), P("leaf"))
    return jax.shard_map(on_device, mesh=mesh, in_specs=placed, out_specs=wide, check_vma=False)
```

time: 34.2 us -> 29.2 us (0.85)
  Pallas kernels: 32.1 us -> 28.3 us
  local copies, waits for them, and re-layouts: 1.87 us -> 0.8 us
    pallas_call x1, Pallas kernels: 32.1 us -> 28.3 us  [on_device(): pl.pallas_call(kernel, out_shape=pltpu.VMEM((C, R, R), BF16), in_specs=[a...]
    unnamed x1, local copies, waits for them, and re-layouts: 1.87 us -> 0.8 us
where the time goes in v2:
time: 29.2 us; the launch traced here: 29.1 us
  Pallas kernels  28.3 us (97%)
  local copies, waits for them, and re-layouts  0.8 us (3%)
    pallas_call x1, Pallas kernels, on_device(): pl.pallas_call(kernel, out_shape=pltpu.VMEM((C, R, R), BF16), in_specs=[a...  28.3 us
    unnamed x1, local copies, waits for them, and re-layouts  0.8 us

profile of v2, /device:TPU:1, one launch (start us, length us, event | category | flops | bytes accessed | tf_op | source)
XLA Modules:
  0.0 29.1 jit_solution(555792552523840363)
XLA Ops:
  0.0 28.3 %shard_map.91 = bf16[32,64,64]{2,1,0:T(8,128)(2,1)S(1)} custom-call(bf16[32,64,64]{2,1,0:T(8,128)(2,1)} %bottom.1, bf16[63,64,64]{2,1,0:T(8,128)(2,1)} %bitcast.10, bf16[6,64,64]{2,1,0:T(8,128)(2,1)} %bitcast.11, bf16[63,16,64,64]{3,2,1,0:T(8,128)(2,1)} %bitcast.8, bf16[7,16,64,64]{3,2,1,0:T(8,128)(2,1)} %bitcast.9, s32[16,63]{1,0:T(8,128)} %bitcast.12, ...), custom_call_target="tpu_custom_call" | custom-call | flops 700000000 | bytes 21000000 | tf_op jit(solution)/shard_map/pallas_call | solution.py:317
  28.3 0.8 %copy.11 = bf16[32,64,64]{2,1,0:T(8,128)(2,1)} copy(bf16[32,64,64]{2,1,0:T(8,128)(2,1)S(1)} %shard_map.91) | data formatting | bytes 524288

commit v3 on v2

--- a/solution.py
+++ b/solution.py
@@ -115,29 +115,30 @@
         n //= 2
     pt[...] = jnp.transpose(mm(f[0], xu[UP])).reshape(2, H, R)
 
+    pl.semaphore_wait(barrier, 2 + (SUB - 1) + (NZ - 1) + (NY - 1))
+
+    def remote(src, dst, ss, rs, peer):
+        return pltpu.make_async_remote_copy(
+            src_ref=src, dst_ref=dst, send_sem=ss, recv_sem=rs, device_id=peer, device_id_type=MESH
+        )
+
+    swap = remote(pt.at[1 - core], pr, core_s.at[0], core_r.at[0], (leaf, chip * 2 + 1 - core))
+    swap.start()
+    get_cs.start()
+
+    for i in range(C):
+        send_b[i] = fold(xb[C + i])
+
+    halo_b = [remote(send_b, recv_b.at[1 - i], halo_s.at[i], halo_r.at[i], sides[i]) for i in range(2)]
+    halo_u = [remote(send_u, recv_u.at[1 - i], halo_s.at[2 + i], halo_r.at[2 + i], sides[i]) for i in range(2)]
+    for copy in halo_b:
+        copy.start()
+
     get_cf.wait()
     ones = lax.broadcasted_iota(jnp.int32, (R, R), 0) == lax.broadcasted_iota(jnp.int32, (R, R), 1)
     lift[pl.ds(0, R)] = ones.astype(F32).astype(BF16)
     lift[pl.ds(R, R)] = cf[2 + chip]
     lift[pl.ds(2 * R, R)] = mm(cf[lax.div(chip, 2)], cf[2 + chip]).astype(BF16)
-    for i in range(C):
-        send_b[i] = fold(xb[C + i])
-
-    pl.semaphore_wait(barrier, 2 + (SUB - 1) + (NZ - 1) + (NY - 1))
-
-    def remote(src, dst, ss, rs, peer):
-        return pltpu.make_async_remote_copy(
-            src_ref=src, dst_ref=dst, send_sem=ss, recv_sem=rs, device_id=peer, device_id_type=MESH
-        )
-
-    swap = remote(pt.at[1 - core], pr, core_s.at[0], core_r.at[0], (leaf, chip * 2 + 1 - core))
-    swap.start()
-    get_cs.start()
-
-    halo_b = [remote(send_b, recv_b.at[1 - i], halo_s.at[i], halo_r.at[i], sides[i]) for i in range(2)]
-    halo_u = [remote(send_u, recv_u.at[1 - i], halo_s.at[2 + i], halo_r.at[2 + i], sides[i]) for i in range(2)]
-    for copy in halo_b:
-        copy.start()
 
     swap.wait_recv()
     node = (pt[pl.ds(core, 1)].reshape(H, R) + pr[...]).astype(BF16)
@@ -169,8 +170,6 @@
 
     for i in range(UP):
         send_u[i] = fold(xu[UP + i])
-    for copy in halo_u:
-        copy.start()
 
     get_part.wait()
     get_count.wait()
@@ -217,6 +216,8 @@
         over_z[i].wait_recv()
         for copy in over_y[i]:
             copy.start()
+    for copy in halo_u:
+        copy.start()
     get_su.start()
 
     for copy in halo_b:
@@ -262,6 +263,7 @@
     y2a = jnp.concatenate([zc[3], zc[4]], axis=1) + mm(y1[:, :R], jnp.concatenate([cf[2], cf[3]], axis=1))
     y2b = jnp.concatenate([zc[5], zc[6]], axis=1) + mm(y1[:, R:], jnp.concatenate([cf[4], cf[5]], axis=1))
     for j, v in enumerate((y2a, y2b)):
+        v = v.astype(BF16)
         ys[2 * j] = fold(v[:, :R])
         ys[2 * j + 1] = fold(v[:, R:])
     lows = [
@@ -301,7 +303,8 @@
 
     for copy in lows:
         copy.wait_recv()
-    halves = [unfold((yr[c] + yr[2 + c]) + (yr[4 + c] + yr[6 + c])) for c in range(2)]
+    sent = yr[...].astype(F32)
+    halves = [unfold((sent[c] + sent[2 + c]) + (sent[4 + c] + sent[6 + c])) for c in range(2)]
     yp = jnp.concatenate(halves, axis=0).astype(BF16)
     far = mm_nt(g[pl.ds(UP, C)].reshape(C * R, R), yp).reshape(C, R, R)
     out[...] = (zb[...] + far).astype(BF16)
@@ -342,8 +345,8 @@
             pltpu.VMEM((3 * H // 2, 2 * R), BF16),
             pltpu.VMEM((NY, NZ, 3 * H // 2, 2 * R), BF16),
             pltpu.VMEM((3 * LEAF + 1, H, R), BF16),
-            pltpu.VMEM((4, H // 2, 2 * R), F32),
-            pltpu.VMEM((SUB, H // 2, 2 * R), F32),
+            pltpu.VMEM((4, H // 2, 2 * R), BF16),
+            pltpu.VMEM((SUB, H // 2, 2 * R), BF16),
             pltpu.VMEM((K, SLOTS), jnp.int32),
             pltpu.VMEM((1, SLOTS), jnp.int32),
             pltpu.VMEM((K, 128), jnp.int32),

time: 29.2 us -> 28.5 us (0.976)
  Pallas kernels: 28.3 us -> 27.6 us
    pallas_call x1, Pallas kernels: 28.3 us -> 27.6 us  [on_device(): pl.pallas_call(kernel, out_shape=pltpu.VMEM((C, R, R), BF16), in_specs=[a...]
where the time goes in v3:
time: 28.5 us; the launch traced here: 28.4 us
  Pallas kernels  27.6 us (97%)
  local copies, waits for them, and re-layouts  0.8 us (3%)
    pallas_call x1, Pallas kernels, on_device(): pl.pallas_call(kernel, out_shape=pltpu.VMEM((C, R, R), BF16), in_specs=[a...  27.6 us
    unnamed x1, local copies, waits for them, and re-layouts  0.8 us

profile of v3, /device:TPU:1, one launch (start us, length us, event | category | flops | bytes accessed | tf_op | source)
XLA Modules:
  0.0 28.4 jit_solution(6709789419359790566)
XLA Ops:
  0.0 27.6 %shard_map.91 = bf16[32,64,64]{2,1,0:T(8,128)(2,1)S(1)} custom-call(bf16[32,64,64]{2,1,0:T(8,128)(2,1)} %bottom.1, bf16[63,64,64]{2,1,0:T(8,128)(2,1)} %bitcast.10, bf16[6,64,64]{2,1,0:T(8,128)(2,1)} %bitcast.11, bf16[63,16,64,64]{3,2,1,0:T(8,128)(2,1)} %bitcast.8, bf16[7,16,64,64]{3,2,1,0:T(8,128)(2,1)} %bitcast.9, s32[16,63]{1,0:T(8,128)} %bitcast.12, ...), custom_call_target="tpu_custom_call" | custom-call | flops 700000000 | bytes 21000000 | tf_op jit(solution)/shard_map/pallas_call | solution.py:320
  27.6 0.8 %copy.11 = bf16[32,64,64]{2,1,0:T(8,128)(2,1)} copy(bf16[32,64,64]{2,1,0:T(8,128)(2,1)S(1)} %shard_map.91) | data formatting | bytes 524288

commit v4 on v3

--- a/solution.py
+++ b/solution.py
@@ -55,7 +55,7 @@
     bottom, transfer, coarse_transfer, coupling, coarse_coupling, partners, counts, coarse_partners, coarse_counts,
     out,
     xb, xu, f, cf, s, cs, cscat, ft, g, w, zb, zu,
-    send_b, send_u, recv_b, recv_u, pt, pr, lift, mine, pool, xc, ys, yr,
+    send_b, send_u, recv_b, recv_u, pt, pr, lift, down, mine, pool, xc, ys, yr,
     part_v, count_v, index_v, index_s, cpart_s, ccount_s, cindex_s,
     load_sem, small_sem, halo_s, halo_r, core_s, core_r, z_s, z_r, y_s, y_r, low_s, low_r,
 ):
@@ -104,9 +104,10 @@
 
     get_x.wait()
     get_fb.wait()
-    get_fu.wait()
     n = C // 2
     while n >= 1:
+        if n == C // 4:
+            get_fu.wait()
         for i in range(n):
             a = 2 * (n + i) - 1
             left = jnp.concatenate([f[a], f[a + 1]], axis=1)
@@ -189,6 +190,12 @@
     to_smem = small(index_v, index_s, 4)
     to_smem.start()
 
+    blank = jnp.zeros((R, 2 * R), BF16)
+    halves = [jnp.concatenate([cf[2 + 2 * j], cf[3 + 2 * j]], axis=1) for j in range(2)]
+    down[pl.ds(0, R)] = jnp.concatenate([halves[0], blank], axis=1)
+    down[pl.ds(R, R)] = jnp.concatenate([blank, halves[1]], axis=1)
+    down[pl.ds(2 * R, R)] = jnp.concatenate([mm(cf[j], halves[j]).astype(BF16) for j in range(2)], axis=1)
+
     g[0] = jnp.transpose(f[0])
     for h in range(1, C):
         ft[h - 1] = jnp.transpose(jnp.concatenate([f[2 * h - 1], f[2 * h]], axis=1))
@@ -256,13 +263,10 @@
     for i in range(7):
         left = jnp.concatenate([xc[cindex_s[i * K + k]] for k in range(K)], axis=1)
         zc.append(mm_nt(left, cscat[i]))
-    y1 = jnp.concatenate([zc[1], zc[2]], axis=1) + mm(
-        zc[0].astype(BF16), jnp.concatenate([cf[0], cf[1]], axis=1)
-    )
-    y1 = y1.astype(BF16)
-    y2a = jnp.concatenate([zc[3], zc[4]], axis=1) + mm(y1[:, :R], jnp.concatenate([cf[2], cf[3]], axis=1))
-    y2b = jnp.concatenate([zc[5], zc[6]], axis=1) + mm(y1[:, R:], jnp.concatenate([cf[4], cf[5]], axis=1))
-    for j, v in enumerate((y2a, y2b)):
+    upper = jnp.concatenate([zc[1], zc[2], zc[0]], axis=1).astype(BF16)
+    y2 = jnp.concatenate(zc[3:], axis=1) + mm(upper, down[...])
+    for j in range(2):
+        v = y2[:, 2 * j * R : 2 * (j + 1) * R]
         v = v.astype(BF16)
         ys[2 * j] = fold(v[:, :R])
         ys[2 * j + 1] = fold(v[:, R:])
@@ -342,6 +346,7 @@
             pltpu.VMEM((2, H, R), F32),
             pltpu.VMEM((H, R), F32),
             pltpu.VMEM((3 * R, R), BF16),
+            pltpu.VMEM((3 * R, 4 * R), BF16),
             pltpu.VMEM((3 * H // 2, 2 * R), BF16),
             pltpu.VMEM((NY, NZ, 3 * H // 2, 2 * R), BF16),
             pltpu.VMEM((3 * LEAF + 1, H, R), BF16),

time: 28.5 us -> 28.4 us (level)
  no operation moved by 1% of the time
where the time goes in v4:
time: 28.4 us; the launch traced here: 28.3 us
  Pallas kernels  27.5 us (97%)
  local copies, waits for them, and re-layouts  0.8 us (3%)
    pallas_call x1, Pallas kernels, on_device(): pl.pallas_call(kernel, out_shape=pltpu.VMEM((C, R, R), BF16), in_specs=[a...  27.5 us
    unnamed x1, local copies, waits for them, and re-layouts  0.8 us

profile of v4, /device:TPU:1, one launch (start us, length us, event | category | flops | bytes accessed | tf_op | source)
XLA Modules:
  0.0 28.3 jit_solution(1243082864672239167)
XLA Ops:
  0.0 27.5 %shard_map.91 = bf16[32,64,64]{2,1,0:T(8,128)(2,1)S(1)} custom-call(bf16[32,64,64]{2,1,0:T(8,128)(2,1)} %bottom.1, bf16[63,64,64]{2,1,0:T(8,128)(2,1)} %bitcast.10, bf16[6,64,64]{2,1,0:T(8,128)(2,1)} %bitcast.11, bf16[63,16,64,64]{3,2,1,0:T(8,128)(2,1)} %bitcast.8, bf16[7,16,64,64]{3,2,1,0:T(8,128)(2,1)} %bitcast.9, s32[16,63]{1,0:T(8,128)} %bitcast.12, ...), custom_call_target="tpu_custom_call" | custom-call | flops 700000000 | bytes 21000000 | tf_op jit(solution)/shard_map/pallas_call | solution.py:324
  27.5 0.8 %copy.11 = bf16[32,64,64]{2,1,0:T(8,128)(2,1)} copy(bf16[32,64,64]{2,1,0:T(8,128)(2,1)S(1)} %shard_map.91) | data formatting | bytes 524288

commit v5 on v4

--- a/solution.py
+++ b/solution.py
@@ -127,13 +127,17 @@
     swap.start()
     get_cs.start()
 
-    for i in range(C):
-        send_b[i] = fold(xb[C + i])
+    for i in range(UP):
+        send_u[i] = fold(xu[UP + i])
 
     halo_b = [remote(send_b, recv_b.at[1 - i], halo_s.at[i], halo_r.at[i], sides[i]) for i in range(2)]
     halo_u = [remote(send_u, recv_u.at[1 - i], halo_s.at[2 + i], halo_r.at[2 + i], sides[i]) for i in range(2)]
-    for copy in halo_b:
-        copy.start()
+    for copy, end in zip(halo_u, (0, DEVICES - 1)):
+
+        @pl.when(me != end)
+        def _():
+            copy.start()
+
 
     get_cf.wait()
     ones = lax.broadcasted_iota(jnp.int32, (R, R), 0) == lax.broadcasted_iota(jnp.int32, (R, R), 1)
@@ -166,11 +170,11 @@
         over_z[i].start()
     for copy in over_y[NZ - 1]:
         copy.start()
-    get_sb.start()
+    get_su.start()
     pool[pl.ds(at_y, 1), pl.ds(at_z, 1)] = mine[...].reshape(1, 1, 3 * H // 2, 2 * R)
 
-    for i in range(UP):
-        send_u[i] = fold(xu[UP + i])
+    for i in range(C):
+        send_b[i] = fold(xb[C + i])
 
     get_part.wait()
     get_count.wait()
@@ -223,27 +227,40 @@
         over_z[i].wait_recv()
         for copy in over_y[i]:
             copy.start()
-    for copy in halo_u:
-        copy.start()
-    get_su.start()
-
-    for copy in halo_b:
-        copy.wait_recv()
+    for copy, end in zip(halo_b, (0, DEVICES - 1)):
+
+        @pl.when(me != end)
+        def _():
+            copy.start()
+
+    get_sb.start()
+
+    for copy, end in zip(halo_u, (DEVICES - 1, 0)):
+
+        @pl.when(me != end)
+        def _():
+            copy.wait_recv()
+
     to_smem.wait()
     for side in range(2):
-        for i in range(C):
-            xb[2 * C * side + i] = unfold(recv_b[side, i])
+        for i in range(UP):
+            xu[2 * UP * side + i] = unfold(recv_u[side, i])
     for side, end in ((0, 0), (1, DEVICES - 1)):
 
         @pl.when(me == end)
         def _():
-            xb[pl.ds(2 * C * side, C)] = jnp.zeros((C, R, R), BF16)
-
-    get_sb.wait()
-
-    @pl.loop(0, C, unroll=C)
+            xu[pl.ds(2 * UP * side, UP)] = jnp.zeros((UP, R, R), BF16)
+
+    get_su.wait()
+
+    @pl.loop(0, UP, unroll=UP)
     def _(i):
-        zb[i] = couple(index_s, 0, UP + i, s, xb)
+        zu[i] = couple(index_s, 0, i, s, xu)
+
+    w[0] = zu[0].astype(BF16)
+    for h in range(1, C // 2):
+        low = zu[pl.ds(2 * h - 1, 2)].reshape(2 * R, R) + mm(ft[h - 1], w[h - 1])
+        w[pl.ds(2 * h - 1, 2)] = low.astype(BF16).reshape(2, R, R)
 
     def spread(y, z):
         at = y * NZ + z
@@ -278,27 +295,26 @@
         copy.start()
     yr[pl.ds(sub, 1)] = ys[pl.ds(lax.div(sub, 2), 1)]
 
-    for copy in halo_u:
-        copy.wait_recv()
+    for copy, end in zip(halo_b, (DEVICES - 1, 0)):
+
+        @pl.when(me != end)
+        def _():
+            copy.wait_recv()
+
     for side in range(2):
-        for i in range(UP):
-            xu[2 * UP * side + i] = unfold(recv_u[side, i])
+        for i in range(C):
+            xb[2 * C * side + i] = unfold(recv_b[side, i])
     for side, end in ((0, 0), (1, DEVICES - 1)):
 
         @pl.when(me == end)
         def _():
-            xu[pl.ds(2 * UP * side, UP)] = jnp.zeros((UP, R, R), BF16)
-
-    get_su.wait()
-
-    @pl.loop(0, UP, unroll=UP)
+            xb[pl.ds(2 * C * side, C)] = jnp.zeros((C, R, R), BF16)
+
+    get_sb.wait()
+
+    @pl.loop(0, C, unroll=C)
     def _(i):
-        zu[i] = couple(index_s, 0, i, s, xu)
-
-    w[0] = zu[0].astype(BF16)
-    for h in range(1, C // 2):
-        low = zu[pl.ds(2 * h - 1, 2)].reshape(2 * R, R) + mm(ft[h - 1], w[h - 1])
-        w[pl.ds(2 * h - 1, 2)] = low.astype(BF16).reshape(2, R, R)
+        zb[i] = couple(index_s, 0, UP + i, s, xb)
 
     for i in range(C // 2):
         h = C // 2 + i
@@ -312,7 +328,19 @@
     yp = jnp.concatenate(halves, axis=0).astype(BF16)
     far = mm_nt(g[pl.ds(UP, C)].reshape(C * R, R), yp).reshape(C, R, R)
     out[...] = (zb[...] + far).astype(BF16)
-    for copy in [swap] + halo_b + halo_u + over_z + sum(over_y, []) + lows:
+    for copy, end in zip(halo_b, (0, DEVICES - 1)):
+
+        @pl.when(me != end)
+        def _():
+            copy.wait_send()
+
+    for copy, end in zip(halo_u, (0, DEVICES - 1)):
+
+        @pl.when(me != end)
+        def _():
+            copy.wait_send()
+
+    for copy in [swap] + over_z + sum(over_y, []) + lows:
         copy.wait_send()
 
 

time: 28.4 us -> 28.4 us (level)
  no operation moved by 1% of the time
where the time goes in v5:
time: 28.4 us; the launch traced here: 28.3 us
  Pallas kernels  27.5 us (97%)
  local copies, waits for them, and re-layouts  0.8 us (3%)
    pallas_call x1, Pallas kernels, on_device(): pl.pallas_call(kernel, out_shape=pltpu.VMEM((C, R, R), BF16), in_specs=[a...  27.5 us
    unnamed x1, local copies, waits for them, and re-layouts  0.8 us

profile of v5, /device:TPU:1, one launch (start us, length us, event | category | flops | bytes accessed | tf_op | source)
XLA Modules:
  0.0 28.3 jit_solution(11890354507637888234)
XLA Ops:
  0.0 27.5 %shard_map.91 = bf16[32,64,64]{2,1,0:T(8,128)(2,1)S(1)} custom-call(bf16[32,64,64]{2,1,0:T(8,128)(2,1)} %bottom.1, bf16[63,64,64]{2,1,0:T(8,128)(2,1)} %bitcast.10, bf16[6,64,64]{2,1,0:T(8,128)(2,1)} %bitcast.11, bf16[63,16,64,64]{3,2,1,0:T(8,128)(2,1)} %bitcast.8, bf16[7,16,64,64]{3,2,1,0:T(8,128)(2,1)} %bitcast.9, s32[16,63]{1,0:T(8,128)} %bitcast.12, ...), custom_call_target="tpu_custom_call" | custom-call | flops 700000000 | bytes 21000000 | tf_op jit(solution)/shard_map/pallas_call | solution.py:352
  27.5 0.8 %copy.11 = bf16[32,64,64]{2,1,0:T(8,128)(2,1)} copy(bf16[32,64,64]{2,1,0:T(8,128)(2,1)S(1)} %shard_map.91) | data formatting | bytes 524288
